TPU v7x, 128 devices: a whole 4x4x4 slice. The times are simulated.
128 devices in a mesh: grp: 8 (over y, core), blk: 16 (over z, x).
Axes of the slice: x: 4, y: 4, z: 4, core: 2. Of those that a mesh axis runs over, the one named last changes fastest.
Arguments:
- embeddings: bfloat16 [49152, 1024], P(('grp', 'blk')), may hold values from -6 to 6
- routes: int32 [49152, 1], P(('grp', 'blk')), may hold values from 0 to 127; in each aligned block of 384 rows (0 to 383, 384 to 767, ...) at most 6 rows name the same one
- ranks: int32 [49152], P(('grp', 'blk')), may hold values from 0 to 49151, each once
Outputs:
- similarity: float32 [49152], P(('grp', 'blk'))
Inputs may be any that keep to these rules, and one draw needn't show every extreme that they name: `routes`: in the rows of one home device, at most 6 documents name the same target, and some home device reaches this bound. `ranks`: A permutation of all document numbers.
All inputs are finite; a program needn't handle non-finite values.
Results may differ from a plain program's by a relative error of at most 0.0013.
Values may be sent and summed in bfloat16 or wider, within the bound.
A program may use at most 128 MiB of HBM per device.

v0:
```python
import jax
import jax.numpy as jnp
from jax import lax
from jax.sharding import PartitionSpec as P


def scores(rows, cols):
    return lax.dot_general(rows, cols, (((1,), (1,)), ((), ())), preferred_element_type=jnp.float32)


def row_best(score, row_rank, col_rank):
    keep = (col_rank[None, :] >= 0) & (col_rank[None, :] < row_rank[:, None])
    return jnp.max(jnp.where(keep, score, jnp.float32(-1.0)), axis=1)


def body(embeddings, routes, ranks):
    count = embeddings.shape[0]
    groups = lax.axis_size("grp")
    blocks = lax.axis_size("blk")
    devices = groups * blocks
    slot = 2 * count // devices
    capacity = devices * slot
    values = embeddings.astype(jnp.float32)
    unit = (values * lax.rsqrt(jnp.sum(values * values, axis=1, keepdims=True) + 1e-06)).astype(
        jnp.bfloat16
    )
    target = routes[:, 0]
    onehot = (target[:, None] == jnp.arange(devices, dtype=jnp.int32)[None, :]).astype(jnp.int32)
    position = jnp.sum(jnp.cumsum(onehot, axis=0) * onehot, axis=1) - 1
    place = target * slot + position
    packing = place[None, :] == jnp.arange(capacity, dtype=jnp.int32)[:, None]
    packed = jnp.dot(packing.astype(jnp.bfloat16), unit, preferred_element_type=jnp.float32).astype(
        jnp.bfloat16
    )
    packed_rank = jnp.max(jnp.where(packing, ranks[None, :], -1), axis=1)
    mine, mine_rank = (
        lax.all_to_all(packed, ("grp", "blk"), split_axis=0, concat_axis=0, tiled=True),
        lax.all_to_all(packed_rank, ("grp", "blk"), split_axis=0, concat_axis=0, tiled=True),
    )
    cols = lax.all_gather(mine, "blk", axis=0, tiled=True)
    col_rank = lax.all_gather(mine_rank, "blk", axis=0, tiled=True)
    total = cols.shape[0]
    step_rows = min(total, capacity)

    def inner(index, best):
        sub = lax.dynamic_slice_in_dim(cols, index * step_rows, step_rows, 0)
        sub_rank = lax.dynamic_slice_in_dim(col_rank, index * step_rows, step_rows, 0)
        return jnp.maximum(best, row_best(scores(mine, sub), mine_rank, sub_rank))

    result = lax.fori_loop(0, total // step_rows, inner, jnp.full((capacity,), -1.0, jnp.float32))
    back = lax.all_to_all(result, ("grp", "blk"), split_axis=0, concat_axis=0, tiled=True)
    return jnp.take(back, place, axis=0)


def solution(mesh):
    in_specs = (P(("grp", "blk"), None), P(("grp", "blk"), None), P(("grp", "blk")))
    out_specs = P(("grp", "blk"))
    return jax.shard_map(body, mesh=mesh, in_specs=in_specs, out_specs=out_specs, check_vma=False)
```

profile of v0, /device:TPU:0, one launch (start us, length us, event | category | flops | bytes accessed | tf_op | source)
XLA Modules:
  0.0 286.1 jit_solution(16061147646031768122)
XLA Ops:
  6.5 0.8 reduce
  7.3 0.1 copy.11
  7.4 0.2 fusion.8
  7.8 0.2 fusion.10
  8.0 0.2 fusion.3
  8.2 2.2 convolution_convert_fusion
  10.5 2.5 all_to_all.27
  13.0 40.8 %all_to_all.36 = bf16[128,6,1024]{2,1,0:T(8,128)(2,1)} all-to-all(bf16[128,6,1024]{2,1,0:T(8,128)(2,1)S(1)} %all_to_all.27), channel_id=1, replica_groups=mesh['grp'=8,'blk'=16] {'grp','blk'}, dimensions={0} | all-to-all | bytes 3145728 | tf_op jit(solution)/shard_map/all_to_all | solution.py:37
  53.7 3.7 %all_to_all.29 = bf16[768,1024]{1,0:T(8,128)(2,1)} reshape(bf16[128,6,1024]{2,1,0:T(8,128)(2,1)} %all_to_all.36) | data formatting | bytes 3145728 | tf_op jit(solution)/shard_map/all_to_all | solution.py:37
  57.5 0.7 copy-done.3
  58.2 0.2 select_reduce_fusion
  58.4 0.8 all_to_all.24
  59.1 4.5 %all-to-all-start = ((s32[128,6,1]{1,2,0:T(1,128)}), s32[128,6,1]{1,2,0:T(1,128)S(1)}, u32[]{:S(2)}, u32[]{:S(2)}) async-start(s32[128,6,1]{1,2,0:T(1,128)} %bitcast.3), calls=%async_computation | async-start | bytes 131072 | tf_op jit(solution)/shard_map/all_to_all | solution.py:38
  63.8 9.4 %all-to-all-done = s32[128,6,1]{1,2,0:T(1,128)S(1)} async-done(((s32[128,6,1]{1,2,0:T(1,128)}), s32[128,6,1]{1,2,0:T(1,128)S(1)}, u32[]{:S(2)}, u32[]{:S(2)}) %all-to-all-start) | async-done | bytes 3104 | tf_op jit(solution)/shard_map/all_to_all | solution.py:38
  73.2 0.5 broadcast.94
  73.7 0.7 reduce.13
  74.4 0.1 reshape.65
  74.6 0.1 all_to_all.26
  74.7 21.7 %all-gather = s32[16,1,768]{2,1,0:T(1,128)S(1)} all-gather(s32[1,1,768]{2,1,0:T(1,128)S(1)} %reshape.65), channel_id=1, replica_groups=mesh['grp'=8,'blk'=16] {'blk'}, dimensions={0}, use_global_device_ids=true | all-gather | bytes 52224 | tf_op jit(solution)/shard_map/all_gather | solution.py:41
  96.4 111.7 %all-gather.3.cloned.1.call-done = bf16[12288,1024]{1,0:T(8,128)(2,1)} async-done(((bf16[768,1024]{1,0:T(8,128)(2,1)}), bf16[12288,1024]{1,0:T(8,128)(2,1)}) %all-gather.3.cloned.1.call-update) | async-done | bytes 25165840 | tf_op jit(solution)/shard_map/all_gather | solution.py:40
  208.1 48.7 %while.14 = (s32[]{:T(128)}, f32[768]{0:T(1024)S(1)}, s32[12288]{0:T(1024)S(1)}, s32[768]{0:T(1024)S(1)}, bf16[12288,1024]{1,0:T(8,128)(2,1)}, /*index=5*/bf16[7...) while((s32[]{:T(128)}, f32[768]{0:T(1024)S(1)}, s32[12288]{0:T(1024)S(1)}, ...), condition=%wide.region_7.8_spmd.clone, body=%wide.region_5.7_spmd.clone.sunk | while | flops 1210320384 | bytes 3172013 | solution.py:50
  208.2 2.9 %fusion.19 = f32[768]{0:T(1024)S(1)} fusion(bf16[768,1024]{1,0:T(8,128)(2,1)S(1)} %get-tuple-element.220, bf16[12288,1024]{1,0:T(8,128)(2,1)} %get-tuple-element.219, s32[]{:T(128)S(6)} %select_n.46, s32[768]{0:T(1024)S(1)} %get-tuple-element.218, s32[768]{0:T(1024)S(1)} %get-tuple-element.193, pred[768]{0:T(1024)(128)(4,1)S(1)} %get-tuple-element.194), kind=kOutput, calls=%fused_computation.2.clone.1 | convolution fusion | flops 1210318080 | bytes 3155716 | tf_op jit(solution)/shard_map/while/body/eval_jaxpr/dot_general | solution.py:8
  211.1 0.1 broadcast_compare_fusion.2
  211.2 2.9 %fusion.19 = f32[768]{0:T(1024)S(1)} fusion(bf16[768,1024]{1,0:T(8,128)(2,1)S(1)} %get-tuple-element.220, bf16[12288,1024]{1,0:T(8,128)(2,1)} %get-tuple-element.219, s32[]{:T(128)S(6)} %select_n.46, s32[768]{0:T(1024)S(1)} %get-tuple-element.218, s32[768]{0:T(1024)S(1)} %get-tuple-element.193, pred[768]{0:T(1024)(128)(4,1)S(1)} %get-tuple-element.194), kind=kOutput, calls=%fused_computation.2.clone.1 | convolution fusion | flops 1210318080 | bytes 3155716 | tf_op jit(solution)/shard_map/while/body/eval_jaxpr/dot_general | solution.py:8
  214.2 2.9 %fusion.19 = f32[768]{0:T(1024)S(1)} fusion(bf16[768,1024]{1,0:T(8,128)(2,1)S(1)} %get-tuple-element.220, bf16[12288,1024]{1,0:T(8,128)(2,1)} %get-tuple-element.219, s32[]{:T(128)S(6)} %select_n.46, s32[768]{0:T(1024)S(1)} %get-tuple-element.218, s32[768]{0:T(1024)S(1)} %get-tuple-element.193, pred[768]{0:T(1024)(128)(4,1)S(1)} %get-tuple-element.194), kind=kOutput, calls=%fused_computation.2.clone.1 | convolution fusion | flops 1210318080 | bytes 3155716 | tf_op jit(solution)/shard_map/while/body/eval_jaxpr/dot_general | solution.py:8
  217.2 0.1 broadcast_compare_fusion.2
  217.3 2.9 %fusion.19 = f32[768]{0:T(1024)S(1)} fusion(bf16[768,1024]{1,0:T(8,128)(2,1)S(1)} %get-tuple-element.220, bf16[12288,1024]{1,0:T(8,128)(2,1)} %get-tuple-element.219, s32[]{:T(128)S(6)} %select_n.46, s32[768]{0:T(1024)S(1)} %get-tuple-element.218, s32[768]{0:T(1024)S(1)} %get-tuple-element.193, pred[768]{0:T(1024)(128)(4,1)S(1)} %get-tuple-element.194), kind=kOutput, calls=%fused_computation.2.clone.1 | convolution fusion | flops 1210318080 | bytes 3155716 | tf_op jit(solution)/shard_map/while/body/eval_jaxpr/dot_general | solution.py:8
  220.2 0.1 broadcast_compare_fusion.2
  220.3 2.9 %fusion.19 = f32[768]{0:T(1024)S(1)} fusion(bf16[768,1024]{1,0:T(8,128)(2,1)S(1)} %get-tuple-element.220, bf16[12288,1024]{1,0:T(8,128)(2,1)} %get-tuple-element.219, s32[]{:T(128)S(6)} %select_n.46, s32[768]{0:T(1024)S(1)} %get-tuple-element.218, s32[768]{0:T(1024)S(1)} %get-tuple-element.193, pred[768]{0:T(1024)(128)(4,1)S(1)} %get-tuple-element.194), kind=kOutput, calls=%fused_computation.2.clone.1 | convolution fusion | flops 1210318080 | bytes 3155716 | tf_op jit(solution)/shard_map/while/body/eval_jaxpr/dot_general | solution.py:8
  223.4 2.9 %fusion.19 = f32[768]{0:T(1024)S(1)} fusion(bf16[768,1024]{1,0:T(8,128)(2,1)S(1)} %get-tuple-element.220, bf16[12288,1024]{1,0:T(8,128)(2,1)} %get-tuple-element.219, s32[]{:T(128)S(6)} %select_n.46, s32[768]{0:T(1024)S(1)} %get-tuple-element.218, s32[768]{0:T(1024)S(1)} %get-tuple-element.193, pred[768]{0:T(1024)(128)(4,1)S(1)} %get-tuple-element.194), kind=kOutput, calls=%fused_computation.2.clone.1 | convolution fusion | flops 1210318080 | bytes 3155716 | tf_op jit(solution)/shard_map/while/body/eval_jaxpr/dot_general | solution.py:8
  226.4 2.9 %fusion.19 = f32[768]{0:T(1024)S(1)} fusion(bf16[768,1024]{1,0:T(8,128)(2,1)S(1)} %get-tuple-element.220, bf16[12288,1024]{1,0:T(8,128)(2,1)} %get-tuple-element.219, s32[]{:T(128)S(6)} %select_n.46, s32[768]{0:T(1024)S(1)} %get-tuple-element.218, s32[768]{0:T(1024)S(1)} %get-tuple-element.193, pred[768]{0:T(1024)(128)(4,1)S(1)} %get-tuple-element.194), kind=kOutput, calls=%fused_computation.2.clone.1 | convolution fusion | flops 1210318080 | bytes 3155716 | tf_op jit(solution)/shard_map/while/body/eval_jaxpr/dot_general | solution.py:8
  229.5 2.9 %fusion.19 = f32[768]{0:T(1024)S(1)} fusion(bf16[768,1024]{1,0:T(8,128)(2,1)S(1)} %get-tuple-element.220, bf16[12288,1024]{1,0:T(8,128)(2,1)} %get-tuple-element.219, s32[]{:T(128)S(6)} %select_n.46, s32[768]{0:T(1024)S(1)} %get-tuple-element.218, s32[768]{0:T(1024)S(1)} %get-tuple-element.193, pred[768]{0:T(1024)(128)(4,1)S(1)} %get-tuple-element.194), kind=kOutput, calls=%fused_computation.2.clone.1 | convolution fusion | flops 1210318080 | bytes 3155716 | tf_op jit(solution)/shard_map/while/body/eval_jaxpr/dot_general | solution.py:8
  232.5 2.9 %fusion.19 = f32[768]{0:T(1024)S(1)} fusion(bf16[768,1024]{1,0:T(8,128)(2,1)S(1)} %get-tuple-element.220, bf16[12288,1024]{1,0:T(8,128)(2,1)} %get-tuple-element.219, s32[]{:T(128)S(6)} %select_n.46, s32[768]{0:T(1024)S(1)} %get-tuple-element.218, s32[768]{0:T(1024)S(1)} %get-tuple-element.193, pred[768]{0:T(1024)(128)(4,1)S(1)} %get-tuple-element.194), kind=kOutput, calls=%fused_computation.2.clone.1 | convolution fusion | flops 1210318080 | bytes 3155716 | tf_op jit(solution)/shard_map/while/body/eval_jaxpr/dot_general | solution.py:8
  235.6 2.9 %fusion.19 = f32[768]{0:T(1024)S(1)} fusion(bf16[768,1024]{1,0:T(8,128)(2,1)S(1)} %get-tuple-element.220, bf16[12288,1024]{1,0:T(8,128)(2,1)} %get-tuple-element.219, s32[]{:T(128)S(6)} %select_n.46, s32[768]{0:T(1024)S(1)} %get-tuple-element.218, s32[768]{0:T(1024)S(1)} %get-tuple-element.193, pred[768]{0:T(1024)(128)(4,1)S(1)} %get-tuple-element.194), kind=kOutput, calls=%fused_computation.2.clone.1 | convolution fusion | flops 1210318080 | bytes 3155716 | tf_op jit(solution)/shard_map/while/body/eval_jaxpr/dot_general | solution.py:8
  238.6 2.9 %fusion.19 = f32[768]{0:T(1024)S(1)} fusion(bf16[768,1024]{1,0:T(8,128)(2,1)S(1)} %get-tuple-element.220, bf16[12288,1024]{1,0:T(8,128)(2,1)} %get-tuple-element.219, s32[]{:T(128)S(6)} %select_n.46, s32[768]{0:T(1024)S(1)} %get-tuple-element.218, s32[768]{0:T(1024)S(1)} %get-tuple-element.193, pred[768]{0:T(1024)(128)(4,1)S(1)} %get-tuple-element.194), kind=kOutput, calls=%fused_computation.2.clone.1 | convolution fusion | flops 1210318080 | bytes 3155716 | tf_op jit(solution)/shard_map/while/body/eval_jaxpr/dot_general | solution.py:8
  241.6 2.9 %fusion.19 = f32[768]{0:T(1024)S(1)} fusion(bf16[768,1024]{1,0:T(8,128)(2,1)S(1)} %get-tuple-element.220, bf16[12288,1024]{1,0:T(8,128)(2,1)} %get-tuple-element.219, s32[]{:T(128)S(6)} %select_n.46, s32[768]{0:T(1024)S(1)} %get-tuple-element.218, s32[768]{0:T(1024)S(1)} %get-tuple-element.193, pred[768]{0:T(1024)(128)(4,1)S(1)} %get-tuple-element.194), kind=kOutput, calls=%fused_computation.2.clone.1 | convolution fusion | flops 1210318080 | bytes 3155716 | tf_op jit(solution)/shard_map/while/body/eval_jaxpr/dot_general | solution.py:8
  244.7 2.9 %fusion.19 = f32[768]{0:T(1024)S(1)} fusion(bf16[768,1024]{1,0:T(8,128)(2,1)S(1)} %get-tuple-element.220, bf16[12288,1024]{1,0:T(8,128)(2,1)} %get-tuple-element.219, s32[]{:T(128)S(6)} %select_n.46, s32[768]{0:T(1024)S(1)} %get-tuple-element.218, s32[768]{0:T(1024)S(1)} %get-tuple-element.193, pred[768]{0:T(1024)(128)(4,1)S(1)} %get-tuple-element.194), kind=kOutput, calls=%fused_computation.2.clone.1 | convolution fusion | flops 1210318080 | bytes 3155716 | tf_op jit(solution)/shard_map/while/body/eval_jaxpr/dot_general | solution.py:8
  247.7 2.9 %fusion.19 = f32[768]{0:T(1024)S(1)} fusion(bf16[768,1024]{1,0:T(8,128)(2,1)S(1)} %get-tuple-element.220, bf16[12288,1024]{1,0:T(8,128)(2,1)} %get-tuple-element.219, s32[]{:T(128)S(6)} %select_n.46, s32[768]{0:T(1024)S(1)} %get-tuple-element.218, s32[768]{0:T(1024)S(1)} %get-tuple-element.193, pred[768]{0:T(1024)(128)(4,1)S(1)} %get-tuple-element.194), kind=kOutput, calls=%fused_computation.2.clone.1 | convolution fusion | flops 1210318080 | bytes 3155716 | tf_op jit(solution)/shard_map/while/body/eval_jaxpr/dot_general | solution.py:8
  250.8 2.9 %fusion.19 = f32[768]{0:T(1024)S(1)} fusion(bf16[768,1024]{1,0:T(8,128)(2,1)S(1)} %get-tuple-element.220, bf16[12288,1024]{1,0:T(8,128)(2,1)} %get-tuple-element.219, s32[]{:T(128)S(6)} %select_n.46, s32[768]{0:T(1024)S(1)} %get-tuple-element.218, s32[768]{0:T(1024)S(1)} %get-tuple-element.193, pred[768]{0:T(1024)(128)(4,1)S(1)} %get-tuple-element.194), kind=kOutput, calls=%fused_computation.2.clone.1 | convolution fusion | flops 1210318080 | bytes 3155716 | tf_op jit(solution)/shard_map/while/body/eval_jaxpr/dot_general | solution.py:8
  253.8 2.9 %fusion.19 = f32[768]{0:T(1024)S(1)} fusion(bf16[768,1024]{1,0:T(8,128)(2,1)S(1)} %get-tuple-element.220, bf16[12288,1024]{1,0:T(8,128)(2,1)} %get-tuple-element.219, s32[]{:T(128)S(6)} %select_n.46, s32[768]{0:T(1024)S(1)} %get-tuple-element.218, s32[768]{0:T(1024)S(1)} %get-tuple-element.193, pred[768]{0:T(1024)(128)(4,1)S(1)} %get-tuple-element.194), kind=kOutput, calls=%fused_computation.2.clone.1 | convolution fusion | flops 1210318080 | bytes 3155716 | tf_op jit(solution)/shard_map/while/body/eval_jaxpr/dot_general | solution.py:8
  256.8 0.8 all_to_all.30
  257.5 8.3 %all-to-all-start.2 = ((f32[128,6,1]{1,2,0:T(1,128)}), f32[128,6,1]{1,2,0:T(1,128)S(1)}, u32[]{:S(2)}, u32[]{:S(2)}) async-start(f32[128,6,1]{1,2,0:T(1,128)} %bitcast.5), calls=%async_computation.2 | async-start | bytes 131072 | tf_op jit(solution)/shard_map/all_to_all | solution.py:51
  265.8 9.5 %all-to-all-done.2 = f32[128,6,1]{1,2,0:T(1,128)S(1)} async-done(((f32[128,6,1]{1,2,0:T(1,128)}), f32[128,6,1]{1,2,0:T(1,128)S(1)}, u32[]{:S(2)}, u32[]{:S(2)}) %all-to-all-start.2) | async-done | bytes 3104 | tf_op jit(solution)/shard_map/all_to_all | solution.py:51
  275.3 0.5 broadcast.95
  275.8 0.8 reduce.14
  276.6 0.1 all_to_all.32
  276.7 1.9 gather_fusion
  278.6 0.6 broadcast_select_fusion
  (48 shorter events, 1.4 us)
Async XLA Ops:
  6.5 1.5 copy-start.1
  6.5 201.5 %all-gather.3.cloned.1.call-start = ((), (), s32[]{:S(2)}) async-start(), calls=%async_computation.3 | async-start | bytes 26738688 | tf_op jit(solution)/shard_map/all_gather | solution.py:40
  57.5 0.7 copy-start.3
  57.5 6.2 %copy-start.2 = (s32[384,1]{0,1:T(1,128)S(1)}, s32[384,1]{0,1:T(1,128)}, u32[]{:S(2)}) copy-start(s32[384,1]{0,1:T(1,128)} %param.6) | copy-start | bytes 4612
  57.5 150.6 %copy-start = (bf16[768,1024]{1,0:T(8,128)(2,1)S(1)}, bf16[768,1024]{1,0:T(8,128)(2,1)}, u32[]{:S(2)}) copy-start(bf16[768,1024]{1,0:T(8,128)(2,1)} %all_to_all.29) | copy-start | bytes 4718596
  59.1 14.0 %all-to-all-start = ((s32[128,6,1]{1,2,0:T(1,128)}), s32[128,6,1]{1,2,0:T(1,128)S(1)}, u32[]{:S(2)}, u32[]{:S(2)}) async-start(s32[128,6,1]{1,2,0:T(1,128)} %bitcast.3), calls=%async_computation | async-start | bytes 131072 | tf_op jit(solution)/shard_map/all_to_all | solution.py:38
  257.5 17.8 %all-to-all-start.2 = ((f32[128,6,1]{1,2,0:T(1,128)}), f32[128,6,1]{1,2,0:T(1,128)S(1)}, u32[]{:S(2)}, u32[]{:S(2)}) async-start(f32[128,6,1]{1,2,0:T(1,128)} %bitcast.5), calls=%async_computation.2 | async-start | bytes 131072 | tf_op jit(solution)/shard_map/all_to_all | solution.py:51
Sparse Core Ops, SparseCore 0:
  57.6 150.3 all-gather.2
where the time goes:
time: 288 us; the launch traced here: 286 us
  waiting for transfers between devices  131 us (45%)
  blocking collectives  62.5 us (22%)
  matrix products  48.9 us (17%)
  between operations  13.5 us (5%)
  starting transfers between devices  12.8 us (4%)
  local copies, waits for them, and re-layouts  11.8 us (4%)
  other arithmetic  5.34 us (2%)
    all_gather x1, waiting for transfers between devices, body(): cols = lax.all_gather(mine, 'blk', axis=0, tiled=True)  112 us
    dot_general x16, matrix products, scores(): lax.dot_general(rows, cols, (((1,), (1,)), ((), ())), preferred_element_t...  46.7 us
    all_to_all x1, blocking collectives, body(): lax.all_to_all(packed, ('grp', 'blk'), split_axis=0, concat_axis=0, tiled...  40.8 us
    all_gather x1, blocking collectives, body(): col_rank = lax.all_gather(mine_rank, 'blk', axis=0, tiled=True)  21.7 us
    all_to_all x1, waiting for transfers between devices, body(): lax.all_to_all(result, ('grp', 'blk'), split_axis=0, concat_axis=0, tiled...  9.45 us
    all_to_all x1, waiting for transfers between devices, body(): lax.all_to_all(packed_rank, ('grp', 'blk'), split_axis=0, concat_axis=0,...  9.42 us
    all_to_all x1, starting transfers between devices, body(): lax.all_to_all(result, ('grp', 'blk'), split_axis=0, concat_axis=0, tiled...  8.29 us
    all_to_all x2, local copies, waits for them, and re-layouts, body(): lax.all_to_all(packed, ('grp', 'blk'), split_axis=0, concat_axis=0, tiled...  6.22 us
  transfers between devices with their start and end apart: 3, of which 3 were waited for; matrix products, arithmetic and copies ran while one was open for 1% of the time, Pallas kernels for 0%

commit v1 on v0

v1 whole, which is shorter than its diff:
```python
import jax
import jax.numpy as jnp
from jax import lax
from jax.experimental import pallas as pl
from jax.experimental.pallas import tpu as pltpu
from jax.sharding import PartitionSpec as P

MESH = pl.DeviceIdType.MESH
D = 1024
DOC = 384
NSLOT = 8
LANES = 128
LATE = float(1 << 20)
DY = (0, 0, 1, 3, 1, 3, 2, 2)
ZZ = (0, 1, 0, 0, 1, 1, 0, 1)
OWN, LEFT, RIGHT, DIAG, BLOCKS = 0, 2, 4, 6, 7


def xor(a, b):
    return a + b - 2 * a * b


def kernel(cap, emb_ref, route_ref, rank_ref, out_ref, unit, pack, send, msg, seen, blk, rks, rcol, rrow, racc, cacc,
           part, rpart, fin, home, s1, r1, sk, rk, sx, rx, sq, rq, sp, rp, sf, rf):
    n = NSLOT * cap
    g, b = lax.axis_index("grp"), lax.axis_index("blk")
    y, k, z, x = g // 2, g % 2, b // 4, b % 4
    o = 1 - k
    zin, zout = z + 1 - 2 * (z % 2), 3 - z
    xp, xm = (x + 1) % 4, (x + 3) % 4
    lsel, rsel = LEFT + xor(k, x // 2), RIGHT + xor(k, z % 2)

    def at(yy, kk, zz, xx):
        return (yy * 2 + kk, zz * 4 + xx)

    def target(i):
        return at((y + DY[i]) % 4, k, zout if ZZ[i] else z, x)

    def source(i):
        return at((y + 4 - DY[i]) % 4, k, zout if ZZ[i] else z, x)

    left, right, sibling, inner = at(y, k, z, xm), at(y, k, z, xp), at(y, o, z, x), at(y, k, zin, x)

    def remote(src, dst, ss, rs, to):
        return pltpu.make_async_remote_copy(src_ref=src, dst_ref=dst, send_sem=ss, recv_sem=rs, device_id=to, device_id_type=MESH)

    barrier = pltpu.get_barrier_semaphore()
    partners = [target(i) for i in range(1, NSLOT)] + [left, right, sibling, inner]
    partners += [at(y, o, z, xm), at(y, o, z, xp), at(y, k, zin, xm), at(y, k, zin, xp)]
    for to in partners:
        pl.semaphore_signal(barrier, inc=1, device_id=to, device_id_type=MESH)

    values = emb_ref[...].astype(jnp.float32)
    unit[...] = (values * lax.rsqrt(jnp.sum(values * values, axis=1, keepdims=True) + 1e-06)).astype(jnp.bfloat16)
    cluster = route_ref[...] // 16
    index = jnp.zeros((1, DOC), jnp.int32)
    for i in range(1, NSLOT):
        zz = zout if ZZ[i] else z
        index = jnp.where(cluster == ((y + DY[i]) % 4) * 2 + zz // 2, i, index)
    chosen = index == lax.broadcasted_iota(jnp.int32, (NSLOT, DOC), 0)
    onehot = jnp.where(chosen, 1.0, 0.0)
    before = lax.broadcasted_iota(jnp.int32, (DOC, DOC), 0) < lax.broadcasted_iota(jnp.int32, (DOC, DOC), 1)
    counts = jnp.dot(onehot.astype(jnp.bfloat16), jnp.where(before, 1.0, 0.0).astype(jnp.bfloat16),
                     preferred_element_type=jnp.float32)
    position = jnp.sum(counts * onehot, axis=0, keepdims=True).astype(jnp.int32)
    place = index * LANES + position
    for i in range(NSLOT):
        hit = place == lax.broadcasted_iota(jnp.int32, (LANES, DOC), 0) + i * LANES
        pack[i * LANES:(i + 1) * LANES, :] = jnp.where(hit, 1.0, 0.0).astype(jnp.bfloat16)

    rank = rank_ref[...]
    line = lax.broadcasted_iota(jnp.int32, (8, DOC), 0)
    digits = jnp.where(line == 0, rank // 256, jnp.where(line == 1, rank % 256, 1)).astype(jnp.float32).astype(jnp.bfloat16)
    placed = lax.dot_general(digits, pack[...], (((1,), (1,)), ((), ())), preferred_element_type=jnp.float32)
    slot_rank = placed[0:1] * 256.0 + placed[1:2] + (1.0 - placed[2:3]) * LATE
    sub, lane = lax.broadcasted_iota(jnp.int32, (8, LANES), 0), lax.broadcasted_iota(jnp.int32, (8, LANES), 1)
    for i in range(NSLOT):
        row = jnp.broadcast_to(slot_rank[:, i * LANES:(i + 1) * LANES], (8, LANES))
        msg[i] = jnp.where((sub == i) & (lane < cap), row, LATE)
    seen[0] = msg[0]

    def rows(i):
        return pl.ds(i * cap, cap)

    first = [None] + [remote(send.at[i], blk.at[OWN + k, rows(i)], s1.at[i], r1.at[i], target(i)) for i in range(1, NSLOT)]
    rank1 = [None] + [remote(msg.at[i], seen.at[i], sk.at[i], rk.at[i], target(i)) for i in range(1, NSLOT)]

    def route(kind, src, dst, to):
        return [remote(blk.at[src, rows(i)], blk.at[dst, rows(i)], sx.at[kind, i], rx.at[kind, i], to) for i in range(NSLOT)], \
            remote(rks.at[src], rks.at[dst], sq.at[kind], rq.at[kind], to)

    to_left, rank_left = route(0, OWN + k, RIGHT + k, left)
    to_right, rank_right = route(1, OWN + k, LEFT + k, right)
    to_sib, rank_sib = route(2, OWN + k, OWN + k, sibling)
    to_inner, rank_inner = route(3, RIGHT + k, DIAG, inner)
    sib_right, rank_sib_right = route(4, RIGHT + k, RIGHT + k, sibling)
    sib_left, rank_sib_left = route(5, LEFT + k, LEFT + k, sibling)

    racc[...] = jnp.full(racc.shape, -1.0, jnp.float32)
    cacc[...] = jnp.full(cacc.shape, -1.0, jnp.float32)
    pl.semaphore_wait(barrier, len(partners))

    for i in range(1, NSLOT):
        rank1[i].start()
    for i in range(NSLOT):
        batch = jnp.dot(pack[i * LANES:i * LANES + cap, :], unit[...], preferred_element_type=jnp.float32).astype(jnp.bfloat16)
        if i == 0:
            blk[OWN + k, 0:cap, :] = batch
            for copies in (to_left, to_right, to_sib):
                copies[0].start()
        else:
            send[i] = batch
            first[i].start()

    def spread(block):
        tile = rks[block]
        for j in range(n // LANES):
            line = jnp.full((8, LANES), LATE, jnp.float32)
            for i in range(NSLOT):
                start = i * cap - j * LANES
                if -cap < start < LANES:
                    piece = jnp.broadcast_to(tile[i:i + 1], (8, LANES))
                    if start % LANES:
                        piece = pltpu.roll(piece, start % LANES, 1)
                    line = jnp.where((lane >= start) & (lane < start + cap), piece, line)
            rcol[block, :, j * LANES:(j + 1) * LANES] = line
            rrow[block, j * LANES:(j + 1) * LANES, :] = jnp.broadcast_to(line[0:1], (LANES, LANES)).T

    for i in range(1, NSLOT):
        rank1[i].wait_recv()
    tile = seen[0]
    for i in range(1, NSLOT):
        tile = jnp.minimum(tile, seen[i])
    rks[OWN + k] = tile
    for copy in (rank_left, rank_right, rank_sib):
        copy.start()
    spread(OWN + k)

    def relay(i):
        to_left[i].wait_recv()
        to_inner[i].start()
        sib_right[i].start()
        to_right[i].wait_recv()
        sib_left[i].start()

    for i in range(1, NSLOT):
        first[i].wait_recv()
        for copies in (to_left, to_right, to_sib):
            copies[i].start()
        if i == 2:
            rank_left.wait_recv()
            rank_inner.start()
            rank_sib_right.start()
            rank_right.wait_recv()
            rank_sib_left.start()
            spread(RIGHT + k)
        if i >= 2:
            relay(i - 2)

    def block_pair(row_block, col_block, start, width, row_start=0, row_count=n, both=True):
        span = pl.ds(row_start, row_count)
        score = lax.dot_general(blk[row_block, span, :], blk[col_block, start:start + width, :], (((1,), (1,)), ((), ())),
                                preferred_element_type=jnp.float32)
        row_rank, best = rrow[row_block, span, :], racc[row_block, span, :]
        for c in range(0, width, LANES):
            col = slice(start + c, start + c + LANES)
            part_score = score[:, c:c + LANES]
            keep = rcol[col_block, 0:1, col] < row_rank
            best = jnp.maximum(best, jnp.where(keep, part_score, -1.0))
            if both:
                rest = jnp.where(keep, -1.0, part_score).reshape(row_count // 8, 8, LANES)
                cacc[col_block, :, col] = jnp.maximum(cacc[col_block, :, col], jnp.max(rest, axis=0))
        racc[row_block, span, :] = best

    chunks = [(c, min(256, n - c)) for c in range(0, n, 256)]

    def covered(c, w):
        return -(-(c + w) // cap)

    for c, w in chunks:
        block_pair(OWN + k, OWN + k, c, w, both=False)

    sib_block = [remote(blk.at[OWN + o, rows(i)], blk.at[OWN + o, rows(i)], sx.at[2, i], rx.at[2, i], sibling) for i in range(NSLOT)]
    rsib = {kind: [remote(blk.at[dst, rows(i)], blk.at[dst, rows(i)], sx.at[kind, i], rx.at[kind, i], sibling) for i in range(NSLOT)]
            for kind, dst in ((4, RIGHT + o), (5, LEFT + o))}
    rsib_rank = {kind: remote(rks.at[dst], rks.at[dst], sq.at[kind], rq.at[kind], sibling)
                 for kind, dst in ((2, OWN + o), (4, RIGHT + o), (5, LEFT + o))}
    rsib_rank[2].wait_recv()
    spread(OWN + o)
    for i in range(NSLOT):
        sib_block[i].wait_recv()
    half = n // 2
    for c, w in chunks:
        block_pair(OWN, OWN + 1, c, w, row_start=pl.multiple_of(k * half, half), row_count=half)

    rank_inner.wait_recv()
    spread(DIAG)
    rsib_rank[4].wait_recv()
    spread(RIGHT + o)
    spread(LEFT + k)
    rsib_rank[5].wait_recv()
    spread(LEFT + o)

    def own_rows(col_block, c, w):
        def step(j, carry):
            block_pair(OWN + j, col_block, c, w)
            return carry
        lax.fori_loop(0, 2, step, 0)

    relayed, arrived = 6, 0
    for c, w in chunks:
        while relayed < covered(c, w):
            relay(relayed)
            relayed += 1
        own_rows(RIGHT + k, c, w)
        if c + w < n:
            while arrived < covered(c, w):
                to_inner[arrived].wait_recv()
                arrived += 1
            own_rows(DIAG, c, w)
    for i in range(NSLOT):
        rsib[4][i].wait_recv()
        rsib[5][i].wait_recv()

    for c, w in chunks:
        block_pair(lsel, RIGHT + k, c, w)

    def side_rows(c, w):
        def step(j, carry):
            block_pair(jnp.where(j == 0, lsel, rsel), DIAG, c, w)
            return carry
        lax.fori_loop(0, 2, step, 0)

    for c, w in chunks:
        if c + w == n:
            while arrived < NSLOT:
                to_inner[arrived].wait_recv()
                arrived += 1
            own_rows(DIAG, c, w)
        side_rows(c, w)

    def folded(block):
        lines = []
        for j in range(n // LANES):
            span = slice(j * LANES, (j + 1) * LANES)
            by_row = jnp.max(racc[block, span, :].T, axis=0, keepdims=True)
            lines.append(jnp.broadcast_to(jnp.maximum(by_row, jnp.max(cacc[block, :, span], axis=0, keepdims=True)), (8, LANES)))
        tile = jnp.full((8, LANES), -1.0, jnp.float32)
        for i in range(NSLOT):
            for j in range(n // LANES):
                start = j * LANES - i * cap
                if -LANES < start < cap:
                    piece = lines[j]
                    if start % LANES:
                        piece = pltpu.roll(piece, start % LANES, 1)
                    tile = jnp.where((sub == i) & (lane >= start) & (lane < min(cap, start + LANES)), piece, tile)
        return tile

    ends = ((OWN + o, sibling, sibling), (lsel, at(y, xor(k, x // 2), z, xm), left), (RIGHT + k, right, left),
            (rsel, at(y, xor(k, z % 2), z, xp), left), (DIAG, at(y, k, zin, xp), left))
    copies = []
    for j, (block, to, _) in enumerate(ends):
        part[j] = folded(block)
        copies.append(remote(part.at[j], rpart.at[j], sp.at[j], rp.at[j], to))
        copies[-1].start()
    best = folded(OWN + k)
    for j, copy in enumerate(copies):
        copy.wait_recv()
        best = jnp.maximum(best, rpart[j])
    fin[...] = best
    back = [None] + [remote(fin, home.at[i], sf.at[i], rf.at[i], source(i)) for i in range(1, NSLOT)]
    for i in range(1, NSLOT):
        back[i].start()
    home[0] = best

    for i in range(NSLOT):
        if i:
            first[i].wait_send()
            rank1[i].wait_send()
        for group in (to_left, to_right, to_sib, to_inner, sib_right, sib_left):
            group[i].wait_send()
    for copy in (rank_left, rank_right, rank_sib, rank_inner, rank_sib_right, rank_sib_left, *copies):
        copy.wait_send()

    lines = []
    for i in range(NSLOT):
        if i:
            back[i].wait_recv()
        value = home[i, i:i + 1, :]
        high = value.astype(jnp.bfloat16).astype(jnp.float32)
        middle = (value - high).astype(jnp.bfloat16).astype(jnp.float32)
        low = value - high - middle
        lines.append(jnp.where(sub == 0, high, jnp.where(sub == 1, middle, jnp.where(sub == 2, low, 0.0))).astype(jnp.bfloat16))
    picked = jnp.dot(jnp.concatenate(lines, axis=1), pack[...], preferred_element_type=jnp.float32)
    out_ref[...] = picked[0:1] + picked[1:2] + picked[2:3]
    for i in range(1, NSLOT):
        back[i].wait_send()


def nearest(cap, embeddings, routes, ranks):
    n = NSLOT * cap
    f32, bf16 = jnp.float32, jnp.bfloat16
    dma = pltpu.SemaphoreType.DMA
    vmem = pl.BlockSpec(memory_space=pltpu.VMEM)
    return pl.pallas_call(
        lambda *refs: kernel(cap, *refs),
        out_shape=jax.ShapeDtypeStruct((1, DOC), f32),
        in_specs=[vmem] * 3,
        out_specs=vmem,
        scratch_shapes=[
            pltpu.VMEM((DOC, D), bf16),
            pltpu.VMEM((NSLOT * LANES, DOC), bf16),
            pltpu.VMEM((NSLOT, cap, D), bf16),
            pltpu.VMEM((NSLOT, 8, LANES), f32),
            pltpu.VMEM((NSLOT, 8, LANES), f32),
            pltpu.VMEM((BLOCKS, n, D), bf16),
            pltpu.VMEM((BLOCKS, 8, LANES), f32),
            pltpu.VMEM((BLOCKS, 8, n), f32),
            pltpu.VMEM((BLOCKS, n, LANES), f32),
            pltpu.VMEM((BLOCKS, n, LANES), f32),
            pltpu.VMEM((BLOCKS, 8, n), f32),
            pltpu.VMEM((5, 8, LANES), f32),
            pltpu.VMEM((5, 8, LANES), f32),
            pltpu.VMEM((8, LANES), f32),
            pltpu.VMEM((NSLOT, 8, LANES), f32),
            dma((NSLOT,)), dma((NSLOT,)), dma((NSLOT,)), dma((NSLOT,)),
            dma((6, NSLOT)), dma((6, NSLOT)), dma((6,)), dma((6,)),
            dma((5,)), dma((5,)), dma((NSLOT,)), dma((NSLOT,)),
        ],
        compiler_params=pltpu.CompilerParams(collective_id=1, has_side_effects=True, vmem_limit_bytes=56 * 2**20),
        cost_estimate=pl.CostEstimate(flops=17 * n * n * D, bytes_accessed=2 * DOC * D, transcendentals=DOC),
    )(embeddings, routes.reshape(1, DOC), ranks.reshape(1, DOC))


def body(embeddings, routes, ranks):
    return nearest(96, embeddings, routes, ranks).reshape(DOC)


def solution(mesh):
    in_specs = (P(("grp", "blk"), None), P(("grp", "blk"), None), P(("grp", "blk")))
    return jax.shard_map(body, mesh=mesh, in_specs=in_specs, out_specs=P(("grp", "blk")), check_vma=False)
```

time: 288 us -> 80.9 us (0.28)
  waiting for transfers between devices: 131 us -> 0 us
  Pallas kernels: 0 us -> 78.2 us
  blocking collectives: 62.5 us -> 0 us
  matrix products: 48.9 us -> 0 us
  between operations: 13.5 us -> 0.01 us
  starting transfers between devices: 12.8 us -> 0 us
  local copies, waits for them, and re-layouts: 11.8 us -> 1.24 us
  other arithmetic: 5.34 us -> 1.28 us
    all_gather x1 -> x0, waiting for transfers between devices: 112 us -> none  [body(): cols = lax.all_gather(mine, 'blk', axis=0, tiled=True)]
    pallas_call x0 -> x1, Pallas kernels: none -> 78.2 us  [nearest(): pl.pallas_call(lambda *refs: kernel(cap, *refs), out_shape=jax.ShapeDtype...]
    dot_general x17 -> x0, matrix products: 48.9 us -> none  [the longest x16 46.7 us: scores(): lax.dot_general(rows, cols, (((1,), (1,)), ((), ())), preferred_element_t...]
    all_to_all x1 -> x0, blocking collectives: 40.8 us -> none  [body(): lax.all_to_all(packed, ('grp', 'blk'), split_axis=0, concat_axis=0, tiled...]
    all_gather x1 -> x0, blocking collectives: 21.7 us -> none  [body(): col_rank = lax.all_gather(mine_rank, 'blk', axis=0, tiled=True)]
    all_to_all x2 -> x0, waiting for transfers between devices: 18.9 us -> none  [the longest x1 9.45 us: body(): lax.all_to_all(result, ('grp', 'blk'), split_axis=0, concat_axis=0, tiled...]
    all_to_all x2 -> x0, starting transfers between devices: 12.8 us -> none  [the longest x1 8.29 us: body(): lax.all_to_all(result, ('grp', 'blk'), split_axis=0, concat_axis=0, tiled...]
    all_to_all x8 -> x0, local copies, waits for them, and re-layouts: 9.01 us -> none  [the longest x2 6.22 us: body(): lax.all_to_all(packed, ('grp', 'blk'), split_axis=0, concat_axis=0, tiled...]
  transfers between devices with their start and end apart: 3 -> 0, of which waited for: 3 -> 0; matrix products, arithmetic and copies ran while one was open for 1% -> 0% of each run, Pallas kernels for 0% -> 0%
where the time goes in v1:
time: 80.9 us; the launch traced here: 80.7 us
  Pallas kernels  78.2 us (97%)
  other arithmetic  1.28 us (2%)
  local copies, waits for them, and re-layouts  1.24 us (2%)
    pallas_call x1, Pallas kernels, nearest(): pl.pallas_call(lambda *refs: kernel(cap, *refs), out_shape=jax.ShapeDtype...  78.2 us

profile of v1, /device:TPU:0, one launch (start us, length us, event | category | flops | bytes accessed | tf_op | source)
XLA Modules:
  0.0 80.7 jit_solution(3023967183193491650)
XLA Ops:
  0.0 1.2 %reshape.10.refs_2_ = s32[1,384]{1,0:T(1,128)} reshape(s32[384]{0:T(512)} %param.5) | data formatting | bytes 3072 | tf_op jit(solution)/shard_map/reshape | solution.py:332
  1.2 78.2 %shard_map.37 = f32[1,384]{1,0:T(1,128)} custom-call(bf16[384,1024]{1,0:T(8,128)(2,1)} %refs_0_.1, s32[1,384]{1,0:T(1,128)} %bitcast.1, s32[1,384]{1,0:T(1,128)} %reshape.10.refs_2_), custom_call_target="tpu_custom_call" | custom-call | flops 10267656192 | bytes 786432 | tf_op jit(solution)/shard_map/pallas_call | solution.py:305
  79.4 1.3 %reduce = f32[384]{0:T(512)} reduce(f32[1,384]{1,0:T(1,128)} %shard_map.37, f32[]{:T(128)} %constant), dimensions={0}, to_apply=%pallas_call.3.reduce_sub_computation | reduce | bytes 3076 | tf_op jit(solution)/shard_map/pallas_call | solution.py:305

commit v2 on v1

--- a/solution.py
+++ b/solution.py
@@ -14,6 +14,12 @@
 DY = (0, 0, 1, 3, 1, 3, 2, 2)
 ZZ = (0, 1, 0, 0, 1, 1, 0, 1)
 OWN, LEFT, RIGHT, DIAG, BLOCKS = 0, 2, 4, 6, 7
+GROUPS = ((0,), (1, 2, 3, 6), (7, 4, 5))
+PIECES = 2
+LAG = 4
+RANKS = 10
+UNITS = tuple((i, p) for group in GROUPS for p in range(PIECES) for i in group)
+FLAG = LANES - 1
 
 
 def xor(a, b):
@@ -64,11 +70,12 @@
                      preferred_element_type=jnp.float32)
     position = jnp.sum(counts * onehot, axis=0, keepdims=True).astype(jnp.int32)
     place = index * LANES + position
+    most = jnp.max(position, axis=1, keepdims=True)
     for i in range(NSLOT):
         hit = place == lax.broadcasted_iota(jnp.int32, (LANES, DOC), 0) + i * LANES
         pack[i * LANES:(i + 1) * LANES, :] = jnp.where(hit, 1.0, 0.0).astype(jnp.bfloat16)
 
-    rank = rank_ref[...]
+    rank = rank_ref[...].reshape(1, DOC)
     line = lax.broadcasted_iota(jnp.int32, (8, DOC), 0)
     digits = jnp.where(line == 0, rank // 256, jnp.where(line == 1, rank % 256, 1)).astype(jnp.float32).astype(jnp.bfloat16)
     placed = lax.dot_general(digits, pack[...], (((1,), (1,)), ((), ())), preferred_element_type=jnp.float32)
@@ -76,17 +83,23 @@
     sub, lane = lax.broadcasted_iota(jnp.int32, (8, LANES), 0), lax.broadcasted_iota(jnp.int32, (8, LANES), 1)
     for i in range(NSLOT):
         row = jnp.broadcast_to(slot_rank[:, i * LANES:(i + 1) * LANES], (8, LANES))
-        msg[i] = jnp.where((sub == i) & (lane < cap), row, LATE)
+        row = jnp.where(lane < cap, row, jnp.where((lane == FLAG) & (most >= cap), -1.0, LATE))
+        msg[i] = jnp.where(sub == i, row, LATE)
     seen[0] = msg[0]
 
-    def rows(i):
-        return pl.ds(i * cap, cap)
-
-    first = [None] + [remote(send.at[i], blk.at[OWN + k, rows(i)], s1.at[i], r1.at[i], target(i)) for i in range(1, NSLOT)]
+    size = cap // PIECES
+
+    def rows(u):
+        i, p = UNITS[u]
+        return pl.ds(i * cap + p * size, size)
+
+    units = range(len(UNITS))
+    first = {u: remote(send.at[pl.ds(i * cap + p * size, size)], blk.at[OWN + k, rows(u)], s1.at[u], r1.at[u], target(i))
+             for u, (i, p) in enumerate(UNITS) if i}
     rank1 = [None] + [remote(msg.at[i], seen.at[i], sk.at[i], rk.at[i], target(i)) for i in range(1, NSLOT)]
 
     def route(kind, src, dst, to):
-        return [remote(blk.at[src, rows(i)], blk.at[dst, rows(i)], sx.at[kind, i], rx.at[kind, i], to) for i in range(NSLOT)], \
+        return [remote(blk.at[src, rows(u)], blk.at[dst, rows(u)], sx.at[kind, u], rx.at[kind, u], to) for u in units], \
             remote(rks.at[src], rks.at[dst], sq.at[kind], rq.at[kind], to)
 
     to_left, rank_left = route(0, OWN + k, RIGHT + k, left)
@@ -96,22 +109,20 @@
     sib_right, rank_sib_right = route(4, RIGHT + k, RIGHT + k, sibling)
     sib_left, rank_sib_left = route(5, LEFT + k, LEFT + k, sibling)
 
-    racc[...] = jnp.full(racc.shape, -1.0, jnp.float32)
-    cacc[...] = jnp.full(cacc.shape, -1.0, jnp.float32)
     pl.semaphore_wait(barrier, len(partners))
 
+    places = jnp.concatenate([pack[i * LANES:i * LANES + cap, :] for i in range(NSLOT)], axis=0)
+    blk[OWN + k, 0:cap, :] = jnp.dot(places[0:cap], unit[...], preferred_element_type=jnp.float32).astype(jnp.bfloat16)
+    for u in range(PIECES):
+        for copies in (to_left, to_right, to_sib):
+            copies[u].start()
+    send[cap:, :] = jnp.dot(places[cap:], unit[...], preferred_element_type=jnp.float32).astype(jnp.bfloat16)
     for i in range(1, NSLOT):
         rank1[i].start()
-    for i in range(NSLOT):
-        batch = jnp.dot(pack[i * LANES:i * LANES + cap, :], unit[...], preferred_element_type=jnp.float32).astype(jnp.bfloat16)
-        if i == 0:
-            blk[OWN + k, 0:cap, :] = batch
-            for copies in (to_left, to_right, to_sib):
-                copies[0].start()
-        else:
-            send[i] = batch
-            first[i].start()
-
+
+    for u in units:
+        if u in first:
+            first[u].start()
     def spread(block):
         tile = rks[block]
         for j in range(n // LANES):
@@ -126,15 +137,15 @@
             rcol[block, :, j * LANES:(j + 1) * LANES] = line
             rrow[block, j * LANES:(j + 1) * LANES, :] = jnp.broadcast_to(line[0:1], (LANES, LANES)).T
 
-    for i in range(1, NSLOT):
-        rank1[i].wait_recv()
-    tile = seen[0]
-    for i in range(1, NSLOT):
-        tile = jnp.minimum(tile, seen[i])
-    rks[OWN + k] = tile
-    for copy in (rank_left, rank_right, rank_sib):
-        copy.start()
-    spread(OWN + k)
+    def combine():
+        for i in range(1, NSLOT):
+            rank1[i].wait_recv()
+        tile = seen[0]
+        for i in range(1, NSLOT):
+            tile = jnp.minimum(tile, seen[i])
+        rks[OWN + k] = tile
+        for copy in (rank_left, rank_right, rank_sib):
+            copy.start()
 
     def relay(i):
         to_left[i].wait_recv()
@@ -143,19 +154,20 @@
         to_right[i].wait_recv()
         sib_left[i].start()
 
-    for i in range(1, NSLOT):
-        first[i].wait_recv()
+    for u in range(PIECES, len(UNITS)):
+        first[u].wait_recv()
         for copies in (to_left, to_right, to_sib):
-            copies[i].start()
-        if i == 2:
+            copies[u].start()
+        if u == RANKS:
+            combine()
+        if u == RANKS + 3:
             rank_left.wait_recv()
             rank_inner.start()
             rank_sib_right.start()
             rank_right.wait_recv()
             rank_sib_left.start()
-            spread(RIGHT + k)
-        if i >= 2:
-            relay(i - 2)
+        if u >= LAG:
+            relay(u - LAG)
 
     def block_pair(row_block, col_block, start, width, row_start=0, row_count=n, both=True):
         span = pl.ds(row_start, row_count)
@@ -175,20 +187,23 @@
     chunks = [(c, min(256, n - c)) for c in range(0, n, 256)]
 
     def covered(c, w):
-        return -(-(c + w) // cap)
-
+        return 1 + max(u for u, (i, p) in enumerate(UNITS) if i * cap + p * size < c + w)
+
+    racc[...] = jnp.full(racc.shape, -1.0, jnp.float32)
+    cacc[...] = jnp.full(cacc.shape, -1.0, jnp.float32)
+    spread(OWN + k)
+    spread(RIGHT + k)
     for c, w in chunks:
         block_pair(OWN + k, OWN + k, c, w, both=False)
 
-    sib_block = [remote(blk.at[OWN + o, rows(i)], blk.at[OWN + o, rows(i)], sx.at[2, i], rx.at[2, i], sibling) for i in range(NSLOT)]
-    rsib = {kind: [remote(blk.at[dst, rows(i)], blk.at[dst, rows(i)], sx.at[kind, i], rx.at[kind, i], sibling) for i in range(NSLOT)]
-            for kind, dst in ((4, RIGHT + o), (5, LEFT + o))}
+    rsib = {kind: [remote(blk.at[dst, rows(u)], blk.at[dst, rows(u)], sx.at[kind, u], rx.at[kind, u], sibling) for u in units]
+            for kind, dst in ((2, OWN + o), (4, RIGHT + o), (5, LEFT + o))}
     rsib_rank = {kind: remote(rks.at[dst], rks.at[dst], sq.at[kind], rq.at[kind], sibling)
                  for kind, dst in ((2, OWN + o), (4, RIGHT + o), (5, LEFT + o))}
     rsib_rank[2].wait_recv()
     spread(OWN + o)
-    for i in range(NSLOT):
-        sib_block[i].wait_recv()
+    for u in units:
+        rsib[2][u].wait_recv()
     half = n // 2
     for c, w in chunks:
         block_pair(OWN, OWN + 1, c, w, row_start=pl.multiple_of(k * half, half), row_count=half)
@@ -207,7 +222,7 @@
             return carry
         lax.fori_loop(0, 2, step, 0)
 
-    relayed, arrived = 6, 0
+    relayed, arrived = len(UNITS) - LAG, 0
     for c, w in chunks:
         while relayed < covered(c, w):
             relay(relayed)
@@ -218,9 +233,9 @@
                 to_inner[arrived].wait_recv()
                 arrived += 1
             own_rows(DIAG, c, w)
-    for i in range(NSLOT):
-        rsib[4][i].wait_recv()
-        rsib[5][i].wait_recv()
+    for u in units:
+        rsib[4][u].wait_recv()
+        rsib[5][u].wait_recv()
 
     for c, w in chunks:
         block_pair(lsel, RIGHT + k, c, w)
@@ -233,11 +248,16 @@
 
     for c, w in chunks:
         if c + w == n:
-            while arrived < NSLOT:
+            while arrived < len(UNITS):
                 to_inner[arrived].wait_recv()
                 arrived += 1
             own_rows(DIAG, c, w)
         side_rows(c, w)
+
+    heard = rks[0]
+    for j in range(1, BLOCKS):
+        heard = jnp.minimum(heard, rks[j])
+    flagged = jnp.min(jnp.min(heard, axis=0, keepdims=True), axis=1, keepdims=True) < 0.0
 
     def folded(block):
         lines = []
@@ -245,7 +265,7 @@
             span = slice(j * LANES, (j + 1) * LANES)
             by_row = jnp.max(racc[block, span, :].T, axis=0, keepdims=True)
             lines.append(jnp.broadcast_to(jnp.maximum(by_row, jnp.max(cacc[block, :, span], axis=0, keepdims=True)), (8, LANES)))
-        tile = jnp.full((8, LANES), -1.0, jnp.float32)
+        tile = jnp.where((lane == FLAG) & flagged, 2.0, -1.0)
         for i in range(NSLOT):
             for j in range(n // LANES):
                 start = j * LANES - i * cap
@@ -273,12 +293,13 @@
         back[i].start()
     home[0] = best
 
-    for i in range(NSLOT):
-        if i:
-            first[i].wait_send()
-            rank1[i].wait_send()
+    for i in range(1, NSLOT):
+        rank1[i].wait_send()
+    for u in units:
+        if u in first:
+            first[u].wait_send()
         for group in (to_left, to_right, to_sib, to_inner, sib_right, sib_left):
-            group[i].wait_send()
+            group[u].wait_send()
     for copy in (rank_left, rank_right, rank_sib, rank_inner, rank_sib_right, rank_sib_left, *copies):
         copy.wait_send()
 
@@ -292,25 +313,27 @@
         low = value - high - middle
         lines.append(jnp.where(sub == 0, high, jnp.where(sub == 1, middle, jnp.where(sub == 2, low, 0.0))).astype(jnp.bfloat16))
     picked = jnp.dot(jnp.concatenate(lines, axis=1), pack[...], preferred_element_type=jnp.float32)
-    out_ref[...] = picked[0:1] + picked[1:2] + picked[2:3]
+    result = picked[0:1] + picked[1:2] + picked[2:3]
+    over = jnp.max(best[0:1, FLAG:], axis=1, keepdims=True)
+    out_ref[...] = jnp.concatenate([result, jnp.broadcast_to(over, (1, LANES))], axis=1).reshape(DOC + LANES)
     for i in range(1, NSLOT):
         back[i].wait_send()
 
 
-def nearest(cap, embeddings, routes, ranks):
+def nearest(cap, number, embeddings, routes, ranks):
     n = NSLOT * cap
     f32, bf16 = jnp.float32, jnp.bfloat16
     dma = pltpu.SemaphoreType.DMA
     vmem = pl.BlockSpec(memory_space=pltpu.VMEM)
     return pl.pallas_call(
         lambda *refs: kernel(cap, *refs),
-        out_shape=jax.ShapeDtypeStruct((1, DOC), f32),
+        out_shape=jax.ShapeDtypeStruct((DOC + LANES,), f32),
         in_specs=[vmem] * 3,
         out_specs=vmem,
         scratch_shapes=[
             pltpu.VMEM((DOC, D), bf16),
             pltpu.VMEM((NSLOT * LANES, DOC), bf16),
-            pltpu.VMEM((NSLOT, cap, D), bf16),
+            pltpu.VMEM((n, D), bf16),
             pltpu.VMEM((NSLOT, 8, LANES), f32),
             pltpu.VMEM((NSLOT, 8, LANES), f32),
             pltpu.VMEM((BLOCKS, n, D), bf16),
@@ -323,17 +346,18 @@
             pltpu.VMEM((5, 8, LANES), f32),
             pltpu.VMEM((8, LANES), f32),
             pltpu.VMEM((NSLOT, 8, LANES), f32),
-            dma((NSLOT,)), dma((NSLOT,)), dma((NSLOT,)), dma((NSLOT,)),
-            dma((6, NSLOT)), dma((6, NSLOT)), dma((6,)), dma((6,)),
+            dma((len(UNITS),)), dma((len(UNITS),)), dma((NSLOT,)), dma((NSLOT,)),
+            dma((6, len(UNITS))), dma((6, len(UNITS))), dma((6,)), dma((6,)),
             dma((5,)), dma((5,)), dma((NSLOT,)), dma((NSLOT,)),
         ],
-        compiler_params=pltpu.CompilerParams(collective_id=1, has_side_effects=True, vmem_limit_bytes=56 * 2**20),
+        compiler_params=pltpu.CompilerParams(collective_id=number, has_side_effects=True, vmem_limit_bytes=56 * 2**20),
         cost_estimate=pl.CostEstimate(flops=17 * n * n * D, bytes_accessed=2 * DOC * D, transcendentals=DOC),
-    )(embeddings, routes.reshape(1, DOC), ranks.reshape(1, DOC))
+    )(embeddings, routes.reshape(1, DOC), ranks)
 
 
 def body(embeddings, routes, ranks):
-    return nearest(96, embeddings, routes, ranks).reshape(DOC)
+    quick = nearest(64, 1, embeddings, routes, ranks)
+    return lax.cond(quick[DOC] > 1.5, lambda: nearest(96, 2, embeddings, routes, ranks)[:DOC], lambda: quick[:DOC])
 
 
 def solution(mesh):

time: 80.9 us -> 59.3 us (0.73)
  Pallas kernels: 78.2 us -> 55.7 us
  other arithmetic: 1.28 us -> 0 us
  local copies, waits for them, and re-layouts: 1.24 us -> 2.46 us
    pallas_call x1, Pallas kernels: 78.2 us -> 55.7 us  [nearest(): pl.pallas_call(lambda *refs: kernel(cap, *refs), out_shape=jax.ShapeDtype...]
    unnamed x0 -> x8, local copies, waits for them, and re-layouts: none -> 1.95 us
    pallas_call x1 -> x0, other arithmetic: 1.28 us -> none  [nearest(): pl.pallas_call(lambda *refs: kernel(cap, *refs), out_shape=jax.ShapeDtype...]
    reshape x1 -> x0, local copies, waits for them, and re-layouts: 1.24 us -> none  [nearest(): ranks.reshape(1, DOC)]
where the time goes in v2:
time: 59.3 us; the launch traced here: 59.1 us
  Pallas kernels  55.7 us (94%)
  local copies, waits for them, and re-layouts  2.46 us (4%)
  between operations  0.68 us (1%)
    pallas_call x1, Pallas kernels, nearest(): pl.pallas_call(lambda *refs: kernel(cap, *refs), out_shape=jax.ShapeDtype...  55.7 us
    unnamed x8, local copies, waits for them, and re-layouts  1.95 us

profile of v2, /device:TPU:0, one launch (start us, length us, event | category | flops | bytes accessed | tf_op | source)
XLA Modules:
  0.0 59.1 jit_solution(3248766713252468513)
XLA Ops:
  0.0 0.0 copy-start.1
  0.0 0.0 copy-start.2
  0.0 0.7 %copy-done.1 = s32[384]{0:T(512)S(1)} copy-done((s32[384]{0:T(512)S(1)}, s32[384]{0:T(512)}, u32[]{:S(2)}) %copy-start.1) | copy-done | bytes 1560
  0.7 0.0 copy-done.2
  0.7 0.0 copy-start
  0.7 55.7 %shard_map.39 = f32[512]{0:T(512)} custom-call(bf16[384,1024]{1,0:T(8,128)(2,1)} %refs_0_.1, s32[1,384]{1,0:T(1,128)S(1)} %bitcast.7, s32[384]{0:T(512)S(1)} %copy-done.1), custom_call_target="tpu_custom_call" | custom-call | flops 4563402752 | bytes 786432 | tf_op jit(solution)/shard_map/pallas_call | solution.py:328
  56.4 0.7 %copy.10 = f32[512]{0:T(512)S(1)} copy(f32[512]{0:T(512)} %shard_map.39) | data formatting | bytes 4096
  57.1 0.5 slice.9
  58.3 0.0 copy-done
  58.3 0.2 conditional.1
  58.5 0.6 copy.11
Async XLA Ops:
  0.0 0.7 %copy-start.1 = (s32[384]{0:T(512)S(1)}, s32[384]{0:T(512)}, u32[]{:S(2)}) copy-start(s32[384]{0:T(512)} %refs_2_.1) | copy-start | bytes 4612
  0.0 0.7 %copy-start.2 = (s32[384,1]{0,1:T(1,128)S(1)}, s32[384,1]{0,1:T(1,128)}, u32[]{:S(2)}) copy-start(s32[384,1]{0,1:T(1,128)} %param.6) | copy-start | bytes 4612
  0.7 57.6 %copy-start = (bf16[384,1024]{1,0:T(8,128)(2,1)S(1)}, bf16[384,1024]{1,0:T(8,128)(2,1)}, u32[]{:S(2)}) copy-start(bf16[384,1024]{1,0:T(8,128)(2,1)} %refs_0_.1) | copy-start | bytes 2359300

commit v3 on v2

--- a/solution.py
+++ b/solution.py
@@ -26,8 +26,8 @@
     return a + b - 2 * a * b
 
 
-def kernel(cap, emb_ref, route_ref, rank_ref, out_ref, unit, pack, send, msg, seen, blk, rks, rcol, rrow, racc, cacc,
-           part, rpart, fin, home, s1, r1, sk, rk, sx, rx, sq, rq, sp, rp, sf, rf):
+def kernel(cap, emb_ref, route_ref, rank_ref, out_ref, flag_ref, unit, pack, send, msg, seen, blk, rks, rcol, rrow, racc, cacc,
+           part, rpart, fin, home, s1, r1, sk, rk, sx, rx, sq, rq, sp, rp, sf, rf, se):
     n = NSLOT * cap
     g, b = lax.axis_index("grp"), lax.axis_index("blk")
     y, k, z, x = g // 2, g % 2, b // 4, b % 4
@@ -50,13 +50,16 @@
     def remote(src, dst, ss, rs, to):
         return pltpu.make_async_remote_copy(src_ref=src, dst_ref=dst, send_sem=ss, recv_sem=rs, device_id=to, device_id_type=MESH)
 
+    load = pltpu.make_async_copy(emb_ref, unit, se)
+    load.start()
     barrier = pltpu.get_barrier_semaphore()
     partners = [target(i) for i in range(1, NSLOT)] + [left, right, sibling, inner]
     partners += [at(y, o, z, xm), at(y, o, z, xp), at(y, k, zin, xm), at(y, k, zin, xp)]
     for to in partners:
         pl.semaphore_signal(barrier, inc=1, device_id=to, device_id_type=MESH)
 
-    values = emb_ref[...].astype(jnp.float32)
+    load.wait()
+    values = unit[...].astype(jnp.float32)
     unit[...] = (values * lax.rsqrt(jnp.sum(values * values, axis=1, keepdims=True) + 1e-06)).astype(jnp.bfloat16)
     cluster = route_ref[...] // 16
     index = jnp.zeros((1, DOC), jnp.int32)
@@ -114,8 +117,9 @@
     places = jnp.concatenate([pack[i * LANES:i * LANES + cap, :] for i in range(NSLOT)], axis=0)
     blk[OWN + k, 0:cap, :] = jnp.dot(places[0:cap], unit[...], preferred_element_type=jnp.float32).astype(jnp.bfloat16)
     for u in range(PIECES):
-        for copies in (to_left, to_right, to_sib):
-            copies[u].start()
+        remote(blk.at[OWN + k, rows(u)], blk.at[DIAG, rows(u)], sx.at[3, u], rx.at[3, u], at(y, k, zin, xm)).start()
+        to_right[u].start()
+        to_sib[u].start()
     send[cap:, :] = jnp.dot(places[cap:], unit[...], preferred_element_type=jnp.float32).astype(jnp.bfloat16)
     for i in range(1, NSLOT):
         rank1[i].start()
@@ -147,12 +151,13 @@
         for copy in (rank_left, rank_right, rank_sib):
             copy.start()
 
-    def relay(i):
-        to_left[i].wait_recv()
-        to_inner[i].start()
-        sib_right[i].start()
-        to_right[i].wait_recv()
-        sib_left[i].start()
+    def relay(u):
+        if u >= PIECES:
+            to_left[u].wait_recv()
+            to_inner[u].start()
+            sib_right[u].start()
+        to_right[u].wait_recv()
+        sib_left[u].start()
 
     for u in range(PIECES, len(UNITS)):
         first[u].wait_recv()
@@ -169,6 +174,22 @@
         if u >= LAG:
             relay(u - LAG)
 
+    def many_rows(row_blocks, col_block, start, width):
+        lines = [cacc[col_block, :, start + c:start + c + LANES] for c in range(0, width, LANES)]
+        for row_block in row_blocks:
+            score = lax.dot_general(blk[row_block], blk[col_block, start:start + width, :], (((1,), (1,)), ((), ())),
+                                    preferred_element_type=jnp.float32)
+            row_rank, best = rrow[row_block], racc[row_block]
+            for j, c in enumerate(range(0, width, LANES)):
+                part_score = score[:, c:c + LANES]
+                keep = rcol[col_block, 0:1, start + c:start + c + LANES] < row_rank
+                best = jnp.maximum(best, jnp.where(keep, part_score, -1.0))
+                rest = jnp.where(keep, -1.0, part_score).reshape(n // 8, 8, LANES)
+                lines[j] = jnp.maximum(lines[j], jnp.max(rest, axis=0))
+            racc[row_block] = best
+        for j, c in enumerate(range(0, width, LANES)):
+            cacc[col_block, :, start + c:start + c + LANES] = lines[j]
+
     def block_pair(row_block, col_block, start, width, row_start=0, row_count=n, both=True):
         span = pl.ds(row_start, row_count)
         score = lax.dot_general(blk[row_block, span, :], blk[col_block, start:start + width, :], (((1,), (1,)), ((), ())),
@@ -189,70 +210,73 @@
     def covered(c, w):
         return 1 + max(u for u, (i, p) in enumerate(UNITS) if i * cap + p * size < c + w)
 
-    racc[...] = jnp.full(racc.shape, -1.0, jnp.float32)
-    cacc[...] = jnp.full(cacc.shape, -1.0, jnp.float32)
-    spread(OWN + k)
-    spread(RIGHT + k)
-    for c, w in chunks:
-        block_pair(OWN + k, OWN + k, c, w, both=False)
+    for u in range(PIECES):
+        to_left[u].start()
 
     rsib = {kind: [remote(blk.at[dst, rows(u)], blk.at[dst, rows(u)], sx.at[kind, u], rx.at[kind, u], sibling) for u in units]
             for kind, dst in ((2, OWN + o), (4, RIGHT + o), (5, LEFT + o))}
     rsib_rank = {kind: remote(rks.at[dst], rks.at[dst], sq.at[kind], rq.at[kind], sibling)
                  for kind, dst in ((2, OWN + o), (4, RIGHT + o), (5, LEFT + o))}
+
+    def own_rows(col_block, c, w):
+        many_rows((OWN, OWN + 1), col_block, c, w)
+
+    relays = list(range(len(UNITS) - LAG, len(UNITS)))
+
+    def relay_next():
+        if relays:
+            relay(relays.pop(0))
+
+    racc[...] = jnp.full(racc.shape, -1.0, jnp.float32)
+    cacc[...] = jnp.full(cacc.shape, -1.0, jnp.float32)
+    spread(OWN + k)
+    for c, w in chunks:
+        relay_next()
+        block_pair(OWN + k, OWN + k, c, w, both=False)
     rsib_rank[2].wait_recv()
     spread(OWN + o)
+    relay_next()
     for u in units:
         rsib[2][u].wait_recv()
     half = n // 2
     for c, w in chunks:
         block_pair(OWN, OWN + 1, c, w, row_start=pl.multiple_of(k * half, half), row_count=half)
-
+    while relays:
+        relay_next()
     rank_inner.wait_recv()
     spread(DIAG)
-    rsib_rank[4].wait_recv()
-    spread(RIGHT + o)
+    early = covered(*chunks[0])
+    for u in range(early):
+        to_inner[u].wait_recv()
+    own_rows(DIAG, *chunks[0])
+    spread(RIGHT + k)
+    for c, w in chunks[1:]:
+        own_rows(RIGHT + k, c, w)
     spread(LEFT + k)
     rsib_rank[5].wait_recv()
     spread(LEFT + o)
-
-    def own_rows(col_block, c, w):
-        def step(j, carry):
-            block_pair(OWN + j, col_block, c, w)
-            return carry
-        lax.fori_loop(0, 2, step, 0)
-
-    relayed, arrived = len(UNITS) - LAG, 0
-    for c, w in chunks:
-        while relayed < covered(c, w):
-            relay(relayed)
-            relayed += 1
-        own_rows(RIGHT + k, c, w)
-        if c + w < n:
-            while arrived < covered(c, w):
-                to_inner[arrived].wait_recv()
-                arrived += 1
-            own_rows(DIAG, c, w)
+    rsib_rank[4].wait_recv()
+    spread(RIGHT + o)
+    for u in units:
+        rsib[5][u].wait_recv()
+    for c, w in chunks[1:]:
+        block_pair(lsel, RIGHT + k, c, w)
+    for u in range(PIECES):
+        to_left[u].wait_recv()
+        sib_right[u].start()
+    own_rows(RIGHT + k, *chunks[0])
+    block_pair(lsel, RIGHT + k, *chunks[0])
     for u in units:
         rsib[4][u].wait_recv()
-        rsib[5][u].wait_recv()
-
-    for c, w in chunks:
-        block_pair(lsel, RIGHT + k, c, w)
 
     def side_rows(c, w):
-        def step(j, carry):
-            block_pair(jnp.where(j == 0, lsel, rsel), DIAG, c, w)
-            return carry
-        lax.fori_loop(0, 2, step, 0)
-
-    for c, w in chunks:
-        if c + w == n:
-            while arrived < len(UNITS):
-                to_inner[arrived].wait_recv()
-                arrived += 1
-            own_rows(DIAG, c, w)
-        side_rows(c, w)
+        many_rows((lsel, rsel), DIAG, c, w)
+
+    side_rows(*chunks[0])
+    for u in units[early:]:
+        to_inner[u].wait_recv()
+    for c, w in chunks[1:]:
+        many_rows((OWN, OWN + 1, lsel, rsel), DIAG, c, w)
 
     heard = rks[0]
     for j in range(1, BLOCKS):
@@ -315,7 +339,8 @@
     picked = jnp.dot(jnp.concatenate(lines, axis=1), pack[...], preferred_element_type=jnp.float32)
     result = picked[0:1] + picked[1:2] + picked[2:3]
     over = jnp.max(best[0:1, FLAG:], axis=1, keepdims=True)
-    out_ref[...] = jnp.concatenate([result, jnp.broadcast_to(over, (1, LANES))], axis=1).reshape(DOC + LANES)
+    out_ref[...] = result.reshape(DOC)
+    flag_ref[...] = jnp.broadcast_to(over, (1, LANES)).reshape(LANES)
     for i in range(1, NSLOT):
         back[i].wait_send()
 
@@ -327,9 +352,9 @@
     vmem = pl.BlockSpec(memory_space=pltpu.VMEM)
     return pl.pallas_call(
         lambda *refs: kernel(cap, *refs),
-        out_shape=jax.ShapeDtypeStruct((DOC + LANES,), f32),
-        in_specs=[vmem] * 3,
-        out_specs=vmem,
+        out_shape=[jax.ShapeDtypeStruct((DOC,), f32), jax.ShapeDtypeStruct((LANES,), f32)],
+        in_specs=[pl.BlockSpec(memory_space=pl.ANY), vmem, vmem],
+        out_specs=[vmem, vmem],
         scratch_shapes=[
             pltpu.VMEM((DOC, D), bf16),
             pltpu.VMEM((NSLOT * LANES, DOC), bf16),
@@ -348,7 +373,7 @@
             pltpu.VMEM((NSLOT, 8, LANES), f32),
             dma((len(UNITS),)), dma((len(UNITS),)), dma((NSLOT,)), dma((NSLOT,)),
             dma((6, len(UNITS))), dma((6, len(UNITS))), dma((6,)), dma((6,)),
-            dma((5,)), dma((5,)), dma((NSLOT,)), dma((NSLOT,)),
+            dma((5,)), dma((5,)), dma((NSLOT,)), dma((NSLOT,)), dma,
         ],
         compiler_params=pltpu.CompilerParams(collective_id=number, has_side_effects=True, vmem_limit_bytes=56 * 2**20),
         cost_estimate=pl.CostEstimate(flops=17 * n * n * D, bytes_accessed=2 * DOC * D, transcendentals=DOC),
@@ -356,8 +381,8 @@
 
 
 def body(embeddings, routes, ranks):
-    quick = nearest(64, 1, embeddings, routes, ranks)
-    return lax.cond(quick[DOC] > 1.5, lambda: nearest(96, 2, embeddings, routes, ranks)[:DOC], lambda: quick[:DOC])
+    quick, flag = nearest(64, 1, embeddings, routes, ranks)
+    return lax.cond(flag[0] > 1.5, lambda: nearest(96, 2, embeddings, routes, ranks)[0], lambda: quick)
 
 
 def solution(mesh):

time: 59.3 us -> 55 us (0.927)
  Pallas kernels: 55.7 us -> 52.6 us
  between operations: 0.68 us -> 0.08 us
    pallas_call x1, Pallas kernels: 55.7 us -> 52.6 us  [nearest(): pl.pallas_call(lambda *refs: kernel(cap, *refs), out_shape=[jax.ShapeDtyp...]
    unnamed x8 -> x9, local copies, waits for them, and re-layouts: 1.95 us -> 1.87 us
where the time goes in v3:
time: 55 us; the launch traced here: 54.8 us
  Pallas kernels  52.6 us (96%)
  local copies, waits for them, and re-layouts  1.87 us (3%)
    pallas_call x1, Pallas kernels, nearest(): pl.pallas_call(lambda *refs: kernel(cap, *refs), out_shape=[jax.ShapeDtyp...  52.6 us
    unnamed x9, local copies, waits for them, and re-layouts  1.87 us

profile of v3, /device:TPU:0, one launch (start us, length us, event | category | flops | bytes accessed | tf_op | source)
XLA Modules:
  0.0 54.8 jit_solution(15807492922648088884)
XLA Ops:
  0.0 0.0 copy-start.1
  0.0 0.0 copy-start.2
  0.0 0.7 %copy-done.1 = s32[384]{0:T(512)S(1)} copy-done((s32[384]{0:T(512)S(1)}, s32[384]{0:T(512)}, u32[]{:S(2)}) %copy-start.1) | copy-done | bytes 1560
  0.7 0.0 copy-done.2
  0.7 0.0 copy-start
  0.7 52.6 %shard_map.39 = (f32[384]{0:T(512)S(1)}, f32[128]{0:T(128)}) custom-call(bf16[384,1024]{1,0:T(8,128)(2,1)} %refs_0_.1, s32[1,384]{1,0:T(1,128)S(1)} %bitcast.4, s32[384]{0:T(512)S(1)} %copy-done.1), custom_call_target="tpu_custom_call" | custom-call | flops 4563402752 | bytes 786432 | tf_op jit(solution)/shard_map/pallas_call | solution.py:353
  53.3 0.0 copy-start.3
  53.3 0.6 %copy-done.3 = f32[128]{0:T(128)S(1)} copy-done((f32[128]{0:T(128)S(1)}, f32[128]{0:T(128)}, u32[]{:S(2)}) %copy-start.3) | copy-done | bytes 536
  54.0 0.0 copy-done
  54.0 0.2 conditional.1
  54.2 0.6 %copy.9 = f32[384]{0:T(512)} copy(f32[384]{0:T(512)S(1)} %get-tuple-element.23) | data formatting | bytes 3072
Async XLA Ops:
  0.0 0.7 %copy-start.1 = (s32[384]{0:T(512)S(1)}, s32[384]{0:T(512)}, u32[]{:S(2)}) copy-start(s32[384]{0:T(512)} %refs_2_.1) | copy-start | bytes 4612
  0.0 0.7 %copy-start.2 = (s32[384,1]{0,1:T(1,128)S(1)}, s32[384,1]{0,1:T(1,128)}, u32[]{:S(2)}) copy-start(s32[384,1]{0,1:T(1,128)} %param.6) | copy-start | bytes 4612
  0.7 53.3 %copy-start = (bf16[384,1024]{1,0:T(8,128)(2,1)S(1)}, bf16[384,1024]{1,0:T(8,128)(2,1)}, u32[]{:S(2)}) copy-start(bf16[384,1024]{1,0:T(8,128)(2,1)} %refs_0_.1) | copy-start | bytes 2359300
  53.3 0.6 %copy-start.3 = (f32[128]{0:T(128)S(1)}, f32[128]{0:T(128)}, u32[]{:S(2)}) copy-start(f32[128]{0:T(128)} %get-tuple-element.21) | copy-start | bytes 1540

commit v4 on v3

--- a/solution.py
+++ b/solution.py
@@ -14,9 +14,9 @@
 DY = (0, 0, 1, 3, 1, 3, 2, 2)
 ZZ = (0, 1, 0, 0, 1, 1, 0, 1)
 OWN, LEFT, RIGHT, DIAG, BLOCKS = 0, 2, 4, 6, 7
-GROUPS = ((0,), (1, 2, 3, 6), (7, 4, 5))
+GROUPS = ((0,), (1, 2, 3, 6), (7, 5, 4))
 PIECES = 2
-LAG = 4
+LAG = 5
 RANKS = 10
 UNITS = tuple((i, p) for group in GROUPS for p in range(PIECES) for i in group)
 FLAG = LANES - 1
@@ -26,7 +26,7 @@
     return a + b - 2 * a * b
 
 
-def kernel(cap, emb_ref, route_ref, rank_ref, out_ref, flag_ref, unit, pack, send, msg, seen, blk, rks, rcol, rrow, racc, cacc,
+def kernel(cap, emb_ref, route_ref, rank_ref, out_ref, flag_ref, routed, ranked, unit, pack, send, msg, seen, blk, rks, rcol, rrow, racc, cacc,
            part, rpart, fin, home, s1, r1, sk, rk, sx, rx, sq, rq, sp, rp, sf, rf, se):
     n = NSLOT * cap
     g, b = lax.axis_index("grp"), lax.axis_index("blk")
@@ -50,18 +50,17 @@
     def remote(src, dst, ss, rs, to):
         return pltpu.make_async_remote_copy(src_ref=src, dst_ref=dst, send_sem=ss, recv_sem=rs, device_id=to, device_id_type=MESH)
 
-    load = pltpu.make_async_copy(emb_ref, unit, se)
-    load.start()
+    loads = [pltpu.make_async_copy(src, dst, se.at[j]) for j, (src, dst) in enumerate(((route_ref, routed), (rank_ref, ranked), (emb_ref, unit)))]
+    for load in loads:
+        load.start()
     barrier = pltpu.get_barrier_semaphore()
     partners = [target(i) for i in range(1, NSLOT)] + [left, right, sibling, inner]
     partners += [at(y, o, z, xm), at(y, o, z, xp), at(y, k, zin, xm), at(y, k, zin, xp)]
     for to in partners:
         pl.semaphore_signal(barrier, inc=1, device_id=to, device_id_type=MESH)
 
-    load.wait()
-    values = unit[...].astype(jnp.float32)
-    unit[...] = (values * lax.rsqrt(jnp.sum(values * values, axis=1, keepdims=True) + 1e-06)).astype(jnp.bfloat16)
-    cluster = route_ref[...] // 16
+    loads[0].wait()
+    cluster = routed[...] // 16
     index = jnp.zeros((1, DOC), jnp.int32)
     for i in range(1, NSLOT):
         zz = zout if ZZ[i] else z
@@ -78,7 +77,8 @@
         hit = place == lax.broadcasted_iota(jnp.int32, (LANES, DOC), 0) + i * LANES
         pack[i * LANES:(i + 1) * LANES, :] = jnp.where(hit, 1.0, 0.0).astype(jnp.bfloat16)
 
-    rank = rank_ref[...].reshape(1, DOC)
+    loads[1].wait()
+    rank = ranked[...].reshape(1, DOC)
     line = lax.broadcasted_iota(jnp.int32, (8, DOC), 0)
     digits = jnp.where(line == 0, rank // 256, jnp.where(line == 1, rank % 256, 1)).astype(jnp.float32).astype(jnp.bfloat16)
     placed = lax.dot_general(digits, pack[...], (((1,), (1,)), ((), ())), preferred_element_type=jnp.float32)
@@ -91,6 +91,10 @@
     seen[0] = msg[0]
 
     size = cap // PIECES
+
+    loads[2].wait()
+    values = unit[...].astype(jnp.float32)
+    unit[...] = (values * lax.rsqrt(jnp.sum(values * values, axis=1, keepdims=True) + 1e-06)).astype(jnp.bfloat16)
 
     def rows(u):
         i, p = UNITS[u]
@@ -257,14 +261,14 @@
     spread(LEFT + o)
     rsib_rank[4].wait_recv()
     spread(RIGHT + o)
+    for u in range(PIECES):
+        to_left[u].wait_recv()
+        sib_right[u].start()
+    own_rows(RIGHT + k, *chunks[0])
     for u in units:
         rsib[5][u].wait_recv()
     for c, w in chunks[1:]:
         block_pair(lsel, RIGHT + k, c, w)
-    for u in range(PIECES):
-        to_left[u].wait_recv()
-        sib_right[u].start()
-    own_rows(RIGHT + k, *chunks[0])
     block_pair(lsel, RIGHT + k, *chunks[0])
     for u in units:
         rsib[4][u].wait_recv()
@@ -300,10 +304,10 @@
                     tile = jnp.where((sub == i) & (lane >= start) & (lane < min(cap, start + LANES)), piece, tile)
         return tile
 
-    ends = ((OWN + o, sibling, sibling), (lsel, at(y, xor(k, x // 2), z, xm), left), (RIGHT + k, right, left),
-            (rsel, at(y, xor(k, z % 2), z, xp), left), (DIAG, at(y, k, zin, xp), left))
+    ends = ((DIAG, at(y, k, zin, xp)), (lsel, at(y, xor(k, x // 2), z, xm)), (RIGHT + k, right),
+            (rsel, at(y, xor(k, z % 2), z, xp)), (OWN + o, sibling))
     copies = []
-    for j, (block, to, _) in enumerate(ends):
+    for j, (block, to) in enumerate(ends):
         part[j] = folded(block)
         copies.append(remote(part.at[j], rpart.at[j], sp.at[j], rp.at[j], to))
         copies[-1].start()
@@ -313,7 +317,7 @@
         best = jnp.maximum(best, rpart[j])
     fin[...] = best
     back = [None] + [remote(fin, home.at[i], sf.at[i], rf.at[i], source(i)) for i in range(1, NSLOT)]
-    for i in range(1, NSLOT):
+    for i in reversed(range(1, NSLOT)):
         back[i].start()
     home[0] = best
 
@@ -335,8 +339,12 @@
         high = value.astype(jnp.bfloat16).astype(jnp.float32)
         middle = (value - high).astype(jnp.bfloat16).astype(jnp.float32)
         low = value - high - middle
-        lines.append(jnp.where(sub == 0, high, jnp.where(sub == 1, middle, jnp.where(sub == 2, low, 0.0))).astype(jnp.bfloat16))
-    picked = jnp.dot(jnp.concatenate(lines, axis=1), pack[...], preferred_element_type=jnp.float32)
+        line = jnp.where(sub == 0, high, jnp.where(sub == 1, middle, jnp.where(sub == 2, low, 0.0)))
+        lines.append(line.astype(jnp.bfloat16))
+        if i % 2:
+            found = jnp.dot(jnp.concatenate(lines, axis=1), pack[(i - 1) * LANES:(i + 1) * LANES, :], preferred_element_type=jnp.float32)
+            picked = found if i == 1 else picked + found
+            lines = []
     result = picked[0:1] + picked[1:2] + picked[2:3]
     over = jnp.max(best[0:1, FLAG:], axis=1, keepdims=True)
     out_ref[...] = result.reshape(DOC)
@@ -353,9 +361,11 @@
     return pl.pallas_call(
         lambda *refs: kernel(cap, *refs),
         out_shape=[jax.ShapeDtypeStruct((DOC,), f32), jax.ShapeDtypeStruct((LANES,), f32)],
-        in_specs=[pl.BlockSpec(memory_space=pl.ANY), vmem, vmem],
+        in_specs=[pl.BlockSpec(memory_space=pl.ANY)] * 3,
         out_specs=[vmem, vmem],
         scratch_shapes=[
+            pltpu.VMEM((1, DOC), jnp.int32),
+            pltpu.VMEM((DOC,), jnp.int32),
             pltpu.VMEM((DOC, D), bf16),
             pltpu.VMEM((NSLOT * LANES, DOC), bf16),
             pltpu.VMEM((n, D), bf16),
@@ -373,7 +383,7 @@
             pltpu.VMEM((NSLOT, 8, LANES), f32),
             dma((len(UNITS),)), dma((len(UNITS),)), dma((NSLOT,)), dma((NSLOT,)),
             dma((6, len(UNITS))), dma((6, len(UNITS))), dma((6,)), dma((6,)),
-            dma((5,)), dma((5,)), dma((NSLOT,)), dma((NSLOT,)), dma,
+            dma((5,)), dma((5,)), dma((NSLOT,)), dma((NSLOT,)), dma((3,)),
         ],
         compiler_params=pltpu.CompilerParams(collective_id=number, has_side_effects=True, vmem_limit_bytes=56 * 2**20),
         cost_estimate=pl.CostEstimate(flops=17 * n * n * D, bytes_accessed=2 * DOC * D, transcendentals=DOC),

time: 55 us -> 54.5 us (level)
  no operation moved by 1% of the time
where the time goes in v4:
time: 54.5 us; the launch traced here: 54.3 us
  Pallas kernels  52.1 us (96%)
  local copies, waits for them, and re-layouts  1.87 us (3%)
    pallas_call x1, Pallas kernels, nearest(): pl.pallas_call(lambda *refs: kernel(cap, *refs), out_shape=[jax.ShapeDtyp...  52.1 us
    unnamed x9, local copies, waits for them, and re-layouts  1.87 us

profile of v4, /device:TPU:0, one launch (start us, length us, event | category | flops | bytes accessed | tf_op | source)
XLA Modules:
  0.0 54.3 jit_solution(15250420068132695858)
XLA Ops:
  0.0 0.0 copy-start.1
  0.0 0.0 copy-start.2
  0.0 0.7 %copy-done.1 = s32[384]{0:T(512)S(1)} copy-done((s32[384]{0:T(512)S(1)}, s32[384]{0:T(512)}, u32[]{:S(2)}) %copy-start.1) | copy-done | bytes 1560
  0.7 0.0 copy-done.2
  0.7 0.0 copy-start
  0.7 52.1 %shard_map.39 = (f32[384]{0:T(512)S(1)}, f32[128]{0:T(128)}) custom-call(bf16[384,1024]{1,0:T(8,128)(2,1)} %refs_0_.1, s32[1,384]{1,0:T(1,128)S(1)} %bitcast.4, s32[384]{0:T(512)S(1)} %copy-done.1), custom_call_target="tpu_custom_call" | custom-call | flops 4563402752 | bytes 786432 | tf_op jit(solution)/shard_map/pallas_call | solution.py:361
  52.8 0.0 copy-start.3
  52.8 0.6 %copy-done.3 = f32[128]{0:T(128)S(1)} copy-done((f32[128]{0:T(128)S(1)}, f32[128]{0:T(128)}, u32[]{:S(2)}) %copy-start.3) | copy-done | bytes 536
  53.5 0.0 copy-done
  53.5 0.2 conditional.1
  53.7 0.6 %copy.9 = f32[384]{0:T(512)} copy(f32[384]{0:T(512)S(1)} %get-tuple-element.23) | data formatting | bytes 3072
Async XLA Ops:
  0.0 0.7 %copy-start.1 = (s32[384]{0:T(512)S(1)}, s32[384]{0:T(512)}, u32[]{:S(2)}) copy-start(s32[384]{0:T(512)} %refs_2_.1) | copy-start | bytes 4612
  0.0 0.7 %copy-start.2 = (s32[384,1]{0,1:T(1,128)S(1)}, s32[384,1]{0,1:T(1,128)}, u32[]{:S(2)}) copy-start(s32[384,1]{0,1:T(1,128)} %param.6) | copy-start | bytes 4612
  0.7 52.8 %copy-start = (bf16[384,1024]{1,0:T(8,128)(2,1)S(1)}, bf16[384,1024]{1,0:T(8,128)(2,1)}, u32[]{:S(2)}) copy-start(bf16[384,1024]{1,0:T(8,128)(2,1)} %refs_0_.1) | copy-start | bytes 2359300
  52.8 0.6 %copy-start.3 = (f32[128]{0:T(128)S(1)}, f32[128]{0:T(128)}, u32[]{:S(2)}) copy-start(f32[128]{0:T(128)} %get-tuple-element.21) | copy-start | bytes 1540

commit v5 on v4

--- a/solution.py
+++ b/solution.py
@@ -361,7 +361,7 @@
     return pl.pallas_call(
         lambda *refs: kernel(cap, *refs),
         out_shape=[jax.ShapeDtypeStruct((DOC,), f32), jax.ShapeDtypeStruct((LANES,), f32)],
-        in_specs=[pl.BlockSpec(memory_space=pl.ANY)] * 3,
+        in_specs=[pl.BlockSpec(memory_space=pltpu.HBM)] * 3,
         out_specs=[vmem, vmem],
         scratch_shapes=[
             pltpu.VMEM((1, DOC), jnp.int32),

time: 54.5 us -> 54.5 us (level)
  no operation moved by 1% of the time
where the time goes in v5:
time: 54.5 us; the launch traced here: 54.3 us
  Pallas kernels  52.1 us (96%)
  local copies, waits for them, and re-layouts  1.87 us (3%)
    pallas_call x1, Pallas kernels, nearest(): pl.pallas_call(lambda *refs: kernel(cap, *refs), out_shape=[jax.ShapeDtyp...  52.1 us
    unnamed x9, local copies, waits for them, and re-layouts  1.87 us

profile of v5, /device:TPU:0, one launch (start us, length us, event | category | flops | bytes accessed | tf_op | source)
XLA Modules:
  0.0 54.3 jit_solution(15250420068132695858)
XLA Ops:
  0.0 0.0 copy-start.1
  0.0 0.0 copy-start.2
  0.0 0.7 %copy-done.1 = s32[384]{0:T(512)S(1)} copy-done((s32[384]{0:T(512)S(1)}, s32[384]{0:T(512)}, u32[]{:S(2)}) %copy-start.1) | copy-done | bytes 1560
  0.7 0.0 copy-done.2
  0.7 0.0 copy-start
  0.7 52.1 %shard_map.39 = (f32[384]{0:T(512)S(1)}, f32[128]{0:T(128)}) custom-call(bf16[384,1024]{1,0:T(8,128)(2,1)} %refs_0_.1, s32[1,384]{1,0:T(1,128)S(1)} %bitcast.4, s32[384]{0:T(512)S(1)} %copy-done.1), custom_call_target="tpu_custom_call" | custom-call | flops 4563402752 | bytes 786432 | tf_op jit(solution)/shard_map/pallas_call | solution.py:361
  52.8 0.0 copy-start.3
  52.8 0.6 %copy-done.3 = f32[128]{0:T(128)S(1)} copy-done((f32[128]{0:T(128)S(1)}, f32[128]{0:T(128)}, u32[]{:S(2)}) %copy-start.3) | copy-done | bytes 536
  53.5 0.0 copy-done
  53.5 0.2 conditional.1
  53.7 0.6 %copy.9 = f32[384]{0:T(512)} copy(f32[384]{0:T(512)S(1)} %get-tuple-element.23) | data formatting | bytes 3072
Async XLA Ops:
  0.0 0.7 %copy-start.1 = (s32[384]{0:T(512)S(1)}, s32[384]{0:T(512)}, u32[]{:S(2)}) copy-start(s32[384]{0:T(512)} %refs_2_.1) | copy-start | bytes 4612
  0.0 0.7 %copy-start.2 = (s32[384,1]{0,1:T(1,128)S(1)}, s32[384,1]{0,1:T(1,128)}, u32[]{:S(2)}) copy-start(s32[384,1]{0,1:T(1,128)} %param.6) | copy-start | bytes 4612
  0.7 52.8 %copy-start = (bf16[384,1024]{1,0:T(8,128)(2,1)S(1)}, bf16[384,1024]{1,0:T(8,128)(2,1)}, u32[]{:S(2)}) copy-start(bf16[384,1024]{1,0:T(8,128)(2,1)} %refs_0_.1) | copy-start | bytes 2359300
  52.8 0.6 %copy-start.3 = (f32[128]{0:T(128)S(1)}, f32[128]{0:T(128)}, u32[]{:S(2)}) copy-start(f32[128]{0:T(128)} %get-tuple-element.21) | copy-start | bytes 1540
